TPU v7x, 256 devices: a whole 4x4x8 slice. The times are simulated.
256 devices in a mesh: xb: 16 (over z, y_lo), fsdp: 16 (over x, y_hi, core).
Axes of the slice: x: 4, y: 4 (y_hi: 2, y_lo: 2; y = y_hi * 2 + y_lo), z: 8, core: 2. Of those that a mesh axis runs over, the one named last changes fastest.
Arguments:
- tokens: bfloat16 [256, 128, 2048], P(('xb', 'fsdp')), may hold values from -24 to 24
- query_weight: bfloat16 [2048, 2048], P('fsdp'), may hold values from -0.125 to 0.125
- current_keys: bfloat16 [256, 128, 2048], P(('xb', 'fsdp')), may hold values from -6 to 6
- current_values: bfloat16 [256, 128, 2048], P(('xb', 'fsdp')), may hold values from -6 to 6
- cache_keys: bfloat16 [256, 512, 2048], P(('xb', 'fsdp')), may hold values from -480 to 480
- cache_values: bfloat16 [256, 512, 2048], P(('xb', 'fsdp')), may hold values from -6 to 6
- cache_fill: int32 [256], P(('xb', 'fsdp')), may hold values from 1 to 512, as said below
- document_group: int32 [256], replicated, may hold values from 0 to 1
- attended_grad: bfloat16 [256, 128, 2048], P(('xb', 'fsdp')), may hold values from -6 to 6
Outputs:
- attended: bfloat16 [256, 128, 2048], P(('xb', 'fsdp'))
- tokens_grad: bfloat16 [256, 128, 2048], P(('xb', 'fsdp'))
- keys_grad: bfloat16 [256, 128, 2048], P(('xb', 'fsdp'))
- values_grad: bfloat16 [256, 128, 2048], P(('xb', 'fsdp'))
- weight_grad: float32 [2048, 2048], P('fsdp')
Inputs may be any that keep to these rules, and one draw needn't show every extreme that they name: `cache_fill`: each document uses the first entries of its cache; some document uses all 512.
All inputs are finite; a program needn't handle non-finite values.
Results may differ from a plain program's by a relative error of at most 0.04.
Values may be sent and summed in bfloat16 or wider, within the bound.
No kernel may reach another device: no remote copies, remote signals or barrier semaphores. Data moves between devices by JAX's collectives and lax.ppermute only.
A program may use at most 128 MiB of HBM per device.

v0:
```python
import jax
import jax.numpy as jnp
from jax import lax
from jax.sharding import PartitionSpec as P

HEADS = 16


NEG = -1e30


def block_forward(query, key_rows, value_rows, key_mask):
    scaling = query.shape[-1] ** (-0.5)
    scores = (
        jnp.einsum("the,khe->thk", query, key_rows, preferred_element_type=jnp.float32) * scaling
    )
    valid = key_mask[:, None, :]
    top_value = jnp.max(jnp.where(valid, scores, NEG), axis=-1)
    weights = jnp.where(valid, jnp.exp(scores - top_value[..., None]), 0.0).astype(jnp.bfloat16)
    totals = jnp.sum(weights.astype(jnp.float32), axis=-1)
    partial_sum = jnp.einsum(
        "thk,khe->the", weights, value_rows, preferred_element_type=jnp.float32
    )
    return (top_value, totals, partial_sum, weights)


def block_backward(weights, factor, grad_out, row_delta, key_rows, value_rows):
    scaling = key_rows.shape[-1] ** (-0.5)
    probs = weights.astype(jnp.float32) * factor[..., None]
    dprob = jnp.einsum("the,khe->thk", grad_out, value_rows, preferred_element_type=jnp.float32)
    slope = (probs * (dprob - row_delta[..., None])).astype(jnp.bfloat16)
    query_part = (
        jnp.einsum("thk,khe->the", slope, key_rows, preferred_element_type=jnp.float32) * scaling
    )
    return (probs, slope, query_part)


def body(
    tokens,
    query_weight,
    current_keys,
    current_values,
    cache_keys,
    cache_values,
    cache_fill,
    document_group,
    attended_grad,
):
    group_size = lax.axis_size("xb")
    shard_count = lax.axis_size("fsdp")
    row_index = lax.axis_index("xb")
    col_index = lax.axis_index("fsdp")
    length = tokens.shape[1]
    full_width = query_weight.shape[1]
    head_width = full_width // HEADS
    cache_len = cache_keys.shape[1]
    inputs = tokens[0]
    full_weight = lax.all_gather(query_weight, "fsdp", axis=0, tiled=True)
    queries = jnp.dot(inputs, full_weight, preferred_element_type=jnp.float32).astype(jnp.bfloat16)
    query = queries.reshape(length, HEADS, head_width)
    own_keys = current_keys[0].reshape(length, HEADS, head_width)
    own_values = current_values[0].reshape(length, HEADS, head_width)
    stale_keys = cache_keys[0].reshape(cache_len, HEADS, head_width)
    stale_values = cache_values[0].reshape(cache_len, HEADS, head_width)
    grid_labels = document_group.reshape(group_size, shard_count)
    labels = jnp.sum(
        jnp.where(jnp.arange(shard_count)[None, :] == col_index, grid_labels, 0), axis=1
    )
    own_label = jnp.sum(jnp.where(jnp.arange(group_size) == row_index, labels, 0))
    positions = jnp.arange(length)
    causal = positions[:, None] >= positions[None, :]
    stale_mask = jnp.broadcast_to(
        (jnp.arange(cache_len) < cache_fill[0])[None, :], (length, cache_len)
    )
    local_fwd = block_forward(query, own_keys, own_values, causal)
    stale_fwd = block_forward(query, stale_keys, stale_values, stale_mask)
    all_keys, all_values = (
        lax.all_gather(current_keys, "xb", axis=0, tiled=True),
        lax.all_gather(current_values, "xb", axis=0, tiled=True),
    )
    peer_keys = all_keys.reshape(group_size * length, HEADS, head_width)
    peer_values = all_values.reshape(group_size * length, HEADS, head_width)
    peer_valid = (labels == own_label) & (jnp.arange(group_size) != row_index)
    cross_mask = jnp.broadcast_to(
        jnp.repeat(peer_valid, length)[None, :], (length, group_size * length)
    )
    cross_top, cross_total, cross_partial, cross_weights = block_forward(
        query, peer_keys, peer_values, cross_mask
    )
    biggest = jnp.maximum(jnp.maximum(local_fwd[0], cross_top), stale_fwd[0])
    local_share = jnp.exp(local_fwd[0] - biggest)
    cross_share = jnp.exp(cross_top - biggest)
    stale_share = jnp.exp(stale_fwd[0] - biggest)
    norm_total = local_share * local_fwd[1] + cross_share * cross_total + stale_share * stale_fwd[1]
    combined = (
        local_share[..., None] * local_fwd[2]
        + cross_share[..., None] * cross_partial
        + stale_share[..., None] * stale_fwd[2]
    )
    attended = (combined / norm_total[..., None]).astype(jnp.bfloat16)
    grad_out = attended_grad[0].reshape(length, HEADS, head_width)
    row_delta = jnp.sum(grad_out.astype(jnp.float32) * attended.astype(jnp.float32), axis=-1)
    cross_factor = cross_share / norm_total
    local_bwd = block_backward(
        local_fwd[3], local_share / norm_total, grad_out, row_delta, own_keys, own_values
    )
    stale_bwd = block_backward(
        stale_fwd[3], stale_share / norm_total, grad_out, row_delta, stale_keys, stale_values
    )
    cross_query = block_backward(
        cross_weights, cross_factor, grad_out, row_delta, peer_keys, peer_values
    )[2]
    query_grad = (
        (local_bwd[2] + cross_query + stale_bwd[2]).astype(jnp.bfloat16).reshape(length, full_width)
    )
    scaling = head_width ** (-0.5)
    keys_grad = (
        jnp.einsum("thk,the->khe", local_bwd[1], query, preferred_element_type=jnp.float32)
        * scaling
    ).astype(jnp.bfloat16)
    local_prob = local_bwd[0].astype(jnp.bfloat16)
    values_grad = jnp.einsum(
        "thk,the->khe", local_prob, grad_out, preferred_element_type=jnp.float32
    ).astype(jnp.bfloat16)
    tokens_grad = jnp.einsum(
        "th,dh->td", query_grad, full_weight, preferred_element_type=jnp.float32
    ).astype(jnp.bfloat16)
    shard_rows = lax.psum_scatter(
        jnp.einsum("tc,th->ch", inputs, query_grad, preferred_element_type=jnp.float32),
        "fsdp",
        scatter_dimension=0,
        tiled=True,
    )
    weight_grad = lax.psum(shard_rows, "xb")
    return (
        attended.reshape(1, length, full_width),
        tokens_grad[None],
        keys_grad.reshape(1, length, full_width),
        values_grad.reshape(1, length, full_width),
        weight_grad,
    )


def solution(mesh):
    in_specs = (
        P(("xb", "fsdp"), None, None),
        P("fsdp", None),
        P(("xb", "fsdp"), None, None),
        P(("xb", "fsdp"), None, None),
        P(("xb", "fsdp"), None, None),
        P(("xb", "fsdp"), None, None),
        P(("xb", "fsdp")),
        P(),
        P(("xb", "fsdp"), None, None),
    )
    out_specs = (
        P(("xb", "fsdp"), None, None),
        P(("xb", "fsdp"), None, None),
        P(("xb", "fsdp"), None, None),
        P(("xb", "fsdp"), None, None),
        P("fsdp", None),
    )
    return jax.shard_map(body, mesh=mesh, in_specs=in_specs, out_specs=out_specs, check_vma=False)
```

profile of v0, /device:TPU:48, one launch (start us, length us, event | category | flops | bytes accessed | tf_op | source)
XLA Modules:
  0.0 843.2 jit_solution(9658356680409327412)
XLA Ops:
  9.5 2.0 copy.142
  12.3 3.9 copy.143
  16.8 3.6 copy.147
  23.9 64.7 %all-gather.4.cloned.1.call-done = bf16[2048,2048]{1,0:T(8,128)(2,1)} async-done(((bf16[128,2048]{1,0:T(8,128)(2,1)}), bf16[2048,2048]{1,0:T(8,128)(2,1)}) %all-gather.4.cloned.1.call-update) | async-done | bytes 8388624 | tf_op jit(solution)/shard_map/all_gather | solution.py:58
  88.5 4.6 convolution_convert_fusion.1
  93.4 179.4 %all-gather.6.cloned.1.call-done = bf16[16,128,2048]{2,1,0:T(8,128)(2,1)} async-done(((bf16[1,128,2048]{2,1,0:T(8,128)(2,1)}), bf16[16,128,2048]{2,1,0:T(8,128)(2,1)}) %all-gather.6.cloned.1.call-update) | async-done | bytes 8388624 | tf_op jit(solution)/shard_map/all_gather | solution.py:78
  272.8 9.8 %copy.144 = bf16[256,8,16,128]{3,2,1,0:T(8,128)(2,1)} copy(bf16[256,8,16,128]{3,1,2,0:T(8,128)(2,1)} %bitcast.139) | data formatting | bytes 16777216
  282.6 12.5 %copy.113 = bf16[2048,16,128]{0,2,1:T(8,128)(2,1)} copy(bf16[2048,16,128]{2,1,0:T(8,128)(2,1)} %bitcast.131) | data formatting | bytes 16777216 | tf_op jit(solution)/shard_map/reshape | solution.py:81
  295.0 163.0 %all-gather.8.cloned.1.call-done = bf16[16,128,2048]{2,1,0:T(8,128)(2,1)} async-done(((bf16[1,128,2048]{2,1,0:T(8,128)(2,1)}), bf16[16,128,2048]{2,1,0:T(8,128)(2,1)}) %all-gather.8.cloned.1.call-update) | async-done | bytes 8388624 | tf_op jit(solution)/shard_map/all_gather | solution.py:79
  458.0 9.8 %copy.146 = bf16[256,8,16,128]{3,2,1,0:T(8,128)(2,1)} copy(bf16[256,8,16,128]{3,1,2,0:T(8,128)(2,1)} %bitcast.140) | data formatting | bytes 16777216
  467.8 12.5 %copy.138 = bf16[2048,16,128]{0,2,1:T(8,128)(2,1)} copy(bf16[2048,16,128]{2,1,0:T(8,128)(2,1)} %bitcast.132) | data formatting | bytes 16777216 | tf_op jit(solution)/shard_map/reshape | solution.py:82
  480.2 5.7 fusion.2
  486.0 5.7 convert_reduce_fusion
  492.6 2.1 convert_reduce_fusion.1
  496.2 6.7 fusion.40
  502.9 3.6 fusion.25
  506.5 3.0 multiply_reduce_fusion
  509.6 1.1 fusion.41
  510.7 12.0 %fusion.6 = f32[16,128,128]{1,2,0:T(8,128)} fusion(bf16[2048,16,128]{0,2,1:T(8,128)(2,1)} %copy.113, bf16[128,16,2048]{2,0,1:T(8,128)(2,1)} %get-tuple-element.33, f32[128,16]{0,1:T(8,128)S(1)} %get-tuple-element.44, f32[128,16]{0,1:T(8,128)S(1)} %get-tuple-element.36, bf16[2048,16,128]{0,2,1:T(8,128)(2,1)} %copy.138, bf16[128,16,128]{0,2,1:T(8,128)(2,1)S(1)} %bitcast.150), kind=kOutput, calls=%fused_computation.12 | convolution fusion | flops 2168455168 | bytes 26755072 | tf_op jit(solution)/shard_map/thk,khe->the/dot_general | solution.py:33
  522.7 6.1 fusion.38
  528.8 2.0 fusion.44
  530.9 8.0 convolution_bitcast_fusion
  539.0 153.9 %reduce-scatter.2.cloned.1.call-done = f32[128,2048]{0,1:T(8,128)} async-done(((f32[2048,2048]{0,1:T(8,128)}), f32[128,2048]{0,1:T(8,128)}) %reduce-scatter.2.cloned.1.call-update) | async-done | bytes 1048592 | tf_op jit(solution)/shard_map/reduce_scatter | solution.py:128
  693.0 1.3 fusion.46
  694.2 1.3 copy.121
  695.6 1.0 copy.124
  696.6 2.0 copy.123
  698.6 1.5 convolution_convert_fusion.2
  700.1 1.0 copy.125
  701.1 7.1 fusion.18
  708.2 125.9 %all-reduce.2.cloned.1.call-done = f32[128,2048]{0,1:T(8,128)} async-done(((f32[128,2048]{0,1:T(8,128)}), f32[128,2048]{0,1:T(8,128)}) %all-reduce.2.cloned.1.call-update) | async-done | bytes 1048592 | tf_op jit(solution)/shard_map/psum | solution.py:134
  834.1 2.5 copy.126
  (51 shorter events, 9.2 us)
Async XLA Ops:
  7.2 81.3 %copy-start = (bf16[1,128,2048]{2,1,0:T(8,128)(2,1)S(1)}, bf16[1,128,2048]{2,1,0:T(8,128)(2,1)}, u32[]{:S(2)}) copy-start(bf16[1,128,2048]{2,1,0:T(8,128)(2,1)} %param.9) | copy-start | bytes 1572868
  7.2 14.3 %copy-start.7 = (bf16[1,128,2048]{2,1,0:T(8,128)(2,1)S(1)}, bf16[1,128,2048]{2,1,0:T(8,128)(2,1)}, u32[]{:S(2)}) copy-start(bf16[1,128,2048]{2,1,0:T(8,128)(2,1)} %param.12) | copy-start | bytes 1572868
  7.2 13.2 %copy-start.8 = (bf16[1,128,2048]{2,1,0:T(8,128)(2,1)S(1)}, bf16[1,128,2048]{2,1,0:T(8,128)(2,1)}, u32[]{:S(2)}) copy-start(bf16[1,128,2048]{2,1,0:T(8,128)(2,1)} %param.17) | copy-start | bytes 1572868
  7.2 81.3 %all-gather.4.cloned.1.call-start = ((), (), s32[]{:S(2)}) async-start(), calls=%async_computation.1 | async-start | bytes 8912896 | tf_op jit(solution)/shard_map/all_gather | solution.py:58
  7.9 264.9 %all-gather.6.cloned.1.call-start = ((), (), s32[]{:S(2)}) async-start(), calls=%async_computation.2 | async-start | bytes 8912896 | tf_op jit(solution)/shard_map/all_gather | solution.py:78
  8.7 449.4 %all-gather.8.cloned.1.call-start = ((), (), s32[]{:S(2)}) async-start(), calls=%async_computation.3 | async-start | bytes 8912896 | tf_op jit(solution)/shard_map/all_gather | solution.py:79
  9.4 683.5 %reduce-scatter.2.cloned.1.call-start = ((), (), s32[]{:S(2)}) async-start(), calls=%async_computation.4 | async-start | bytes 17825792 | tf_op jit(solution)/shard_map/reduce_scatter | solution.py:128
  485.9 5.7 copy-start.1
  491.6 3.1 copy-start.2
  491.6 4.5 slice-start
  492.6 3.7 slice-start.1
  502.9 6.7 copy-start.4
  502.9 6.7 copy-start.6
  502.9 6.7 copy-start.9
  522.7 6.2 copy-start.3
  538.9 154.0 %copy-start.5 = (bf16[128,16,128]{0,2,1:T(8,128)(2,1)S(1)}, bf16[128,16,128]{0,2,1:T(8,128)(2,1)}, u32[]{:S(2)}) copy-start(bf16[128,16,128]{0,2,1:T(8,128)(2,1)} %fusion.41) | copy-start | bytes 1572868
  538.9 295.2 %all-reduce.2.cloned.1.call-start = ((), (), s32[]{:S(2)}) async-start(), calls=%async_computation.5 | async-start | bytes 2097152 | tf_op jit(solution)/shard_map/psum | solution.py:134
Sparse Core Ops, SparseCore 0:
  10.7 77.7 all-gather.3
  90.3 182.4 all-gather.5
  274.6 183.3 all-gather.7
  539.1 153.8 reduce-scatter.1
  695.6 138.5 all-reduce.1
where the time goes:
time: 846 us; the launch traced here: 843 us
  waiting for transfers between devices  689 us (81%)
  local copies, waits for them, and re-layouts  65 us (8%)
  matrix products  64.1 us (8%)
  between operations  14.6 us (2%)
  other arithmetic  10.3 us (1%)
    all_gather x1, waiting for transfers between devices, body(): lax.all_gather(current_keys, 'xb', axis=0, tiled=True)  179 us
    all_gather x1, waiting for transfers between devices, body(): lax.all_gather(current_values, 'xb', axis=0, tiled=True)  163 us
    reduce_scatter x1, waiting for transfers between devices, body(): lax.psum_scatter(jnp.einsum('tc,th->ch', inputs, query_grad, preferred_el...  154 us
    psum x1, waiting for transfers between devices, body(): weight_grad = lax.psum(shard_rows, 'xb')  126 us
    all_gather x1, waiting for transfers between devices, body(): full_weight = lax.all_gather(query_weight, 'fsdp', axis=0, tiled=True)  64.7 us
    unnamed x33, local copies, waits for them, and re-layouts  31.7 us
    dot_general x3, matrix products, block_backward(): jnp.einsum('thk,khe->the', slope, key_rows, preferred_element_type=jnp.fl...  20.1 us
  transfers between devices with their start and end apart: 5, of which 5 were waited for; matrix products, arithmetic and copies ran while one was open for 7% of the time, Pallas kernels for 0%

commit v1 on v0

v1 whole, which is shorter than its diff:
```python
import functools

import jax
import jax.numpy as jnp
from jax import lax
from jax.experimental import pallas as pl
from jax.experimental.pallas import tpu as pltpu
from jax.sharding import Mesh
from jax.sharding import PartitionSpec as P

HEADS = 16
HEAD = 128
SEQ = 128
NEG = -1e30
FLOOR = -1e29
SCALING = HEAD ** (-0.5)
LOG2E = 1.4426950408889634
XB = ("g", "q")
FS = ("x", "yh", "core")
BF = jnp.bfloat16
F32 = jnp.float32


def dot_nt(a, b):
    return lax.dot_general(a, b, (((1,), (1,)), ((), ())), preferred_element_type=F32)


def dot_nn(a, b):
    return lax.dot_general(a, b, (((1,), (0,)), ((), ())), preferred_element_type=F32)


def split3(x):
    hi = x.astype(BF)
    rest = x - hi.astype(F32)
    mid = rest.astype(BF)
    low = (rest - mid.astype(F32)).astype(BF)
    return hi, mid, low


def stat_rows(columns):
    lane = lax.broadcasted_iota(jnp.int32, (SEQ, SEQ), 1)
    tile = jnp.zeros((SEQ, SEQ), F32)
    for i, column in enumerate(columns):
        tile = jnp.where(lane == i, column, tile)
    return tile.T


def cross_kernel(q_ref, kvg_ref, g_ref, bias_ref, out_ref, k_s, v_s, kv_s):
    docs = kvg_ref.shape[0]

    @pl.when(pl.program_id(0) == 0)
    def _():
        for m in range(docs):
            k = kvg_ref[m, 0]
            v = kvg_ref[m, 1]
            k_s[m * SEQ : (m + 1) * SEQ, :] = k
            v_s[m * SEQ : (m + 1) * SEQ, :] = v
            kv_s[m * SEQ : (m + 1) * SEQ, :HEAD] = v
            kv_s[m * SEQ : (m + 1) * SEQ, HEAD:] = k

    for j in range(q_ref.shape[0]):
        q = q_ref[j]
        g = g_ref[j, 0]
        scores = dot_nt(q, k_s[...]) * (SCALING * LOG2E) + bias_ref[j]
        top = jnp.maximum(jnp.max(scores, axis=1, keepdims=True), FLOOR)
        weights = jnp.exp2(scores - top).astype(BF)
        weights32 = weights.astype(F32)
        total = jnp.sum(weights32, axis=1, keepdims=True)
        inverse = 1.0 / jnp.maximum(total, 0.5)
        both = dot_nn(weights, kv_s[...]) * inverse
        o = both[:, :HEAD]
        delta = jnp.sum(o * g.astype(F32), axis=1, keepdims=True)
        slope = (weights32 * (dot_nt(g, v_s[...]) - delta)).astype(BF)
        a = dot_nn(slope, k_s[...]) * inverse
        out_ref[j, 0:SEQ, :] = o.astype(BF)
        out_ref[j, SEQ : 2 * SEQ, :] = a.astype(BF)
        out_ref[j, 2 * SEQ : 3 * SEQ, :] = both[:, HEAD:].astype(BF)
        top = jnp.where(total > 0.0, top, NEG)
        rows = stat_rows([top, total, delta])[0:8, :]
        hi, mid, low = split3(rows)
        out_ref[j, 3 * SEQ : 3 * SEQ + 16, :] = jnp.concatenate(
            [hi.astype(F32), mid.astype(F32)], axis=0
        ).astype(BF)
        out_ref[j, 3 * SEQ + 16 : 3 * SEQ + 32, :] = jnp.concatenate(
            [low.astype(F32), jnp.zeros((8, SEQ), F32)], axis=0
        ).astype(BF)


def cross_attention(q_heads, kvg, bias):
    docs = q_heads.shape[0]
    step = 2
    return pl.pallas_call(
        cross_kernel,
        grid=(docs // step,),
        in_specs=[
            pl.BlockSpec((step, SEQ, HEAD), lambda i: (i, 0, 0)),
            pl.BlockSpec((docs, 2, SEQ, HEAD), lambda i: (0, 0, 0, 0)),
            pl.BlockSpec((step, 1, SEQ, HEAD), lambda i: (i, 2, 0, 0)),
            pl.BlockSpec((step, 1, docs * SEQ), lambda i: (i, 0, 0)),
        ],
        out_specs=pl.BlockSpec((step, 3 * SEQ + 32, HEAD), lambda i: (i, 0, 0)),
        out_shape=jax.ShapeDtypeStruct((docs, 3 * SEQ + 32, HEAD), BF),
        scratch_shapes=[
            pltpu.VMEM((docs * SEQ, HEAD), BF),
            pltpu.VMEM((docs * SEQ, HEAD), BF),
            pltpu.VMEM((docs * SEQ, 2 * HEAD), BF),
        ],
        compiler_params=pltpu.CompilerParams(vmem_limit_bytes=40 * 2**20),
        cost_estimate=pl.CostEstimate(
            flops=10 * docs * docs * SEQ * SEQ * HEAD,
            bytes_accessed=4 * 2**20,
            transcendentals=docs * docs * SEQ * SEQ,
        ),
        name="cross",
    )(q_heads, kvg, kvg, bias)


def own_kernel(fill_ref, q_ref, g_ref, ck_ref, cv_ref, lk_ref, lv_ref, o_ref, a_ref, b_ref, s_ref):
    q = q_ref[0]
    g = g_ref[0]
    cache = ck_ref.shape[1]
    entry = lax.broadcasted_iota(jnp.int32, (SEQ, cache), 1)
    row = lax.broadcasted_iota(jnp.int32, (SEQ, SEQ), 0)
    col = lax.broadcasted_iota(jnp.int32, (SEQ, SEQ), 1)
    stale = jnp.where(
        entry < fill_ref[0], dot_nt(q, ck_ref[0]) * (SCALING * LOG2E), NEG
    )
    local = jnp.where(col <= row, dot_nt(q, lk_ref[0]) * (SCALING * LOG2E), NEG)
    top = jnp.maximum(
        jnp.max(stale, axis=1, keepdims=True), jnp.max(local, axis=1, keepdims=True)
    )
    ws = jnp.exp2(stale - top).astype(BF)
    wl = jnp.exp2(local - top).astype(BF)
    ws32 = ws.astype(F32)
    wl32 = wl.astype(F32)
    total = jnp.sum(ws32, axis=1, keepdims=True) + jnp.sum(wl32, axis=1, keepdims=True)
    inverse = 1.0 / total
    o = (dot_nn(ws, cv_ref[0]) + dot_nn(wl, lv_ref[0])) * inverse
    b = (dot_nn(ws, ck_ref[0]) + dot_nn(wl, lk_ref[0])) * inverse
    delta = jnp.sum(o * g.astype(F32), axis=1, keepdims=True)
    ss = (ws32 * (dot_nt(g, cv_ref[0]) - delta)).astype(BF)
    sl = (wl32 * (dot_nt(g, lv_ref[0]) - delta)).astype(BF)
    o_ref[...] = o
    a_ref[...] = (dot_nn(ss, ck_ref[0]) + dot_nn(sl, lk_ref[0])) * inverse
    b_ref[...] = b
    s_ref[0] = stat_rows([top, total, delta])[0:8, :]


def own_attention(fill, q_own, grad, cache_k, cache_v, local_k, local_v):
    cache = cache_k.shape[1]
    width = HEADS * HEAD
    head_block = pl.BlockSpec((1, SEQ, HEAD), lambda h, f: (0, 0, h))
    cache_block = pl.BlockSpec((1, cache, HEAD), lambda h, f: (0, 0, h))
    out_block = pl.BlockSpec((SEQ, HEAD), lambda h, f: (0, h))
    return pl.pallas_call(
        own_kernel,
        grid_spec=pltpu.PrefetchScalarGridSpec(
            num_scalar_prefetch=1,
            grid=(HEADS,),
            in_specs=[
                pl.BlockSpec((1, SEQ, HEAD), lambda h, f: (h % 4, 0, h // 4)),
                head_block,
                cache_block,
                cache_block,
                head_block,
                head_block,
            ],
            out_specs=[
                out_block,
                out_block,
                out_block,
                pl.BlockSpec((1, 8, SEQ), lambda h, f: (h, 0, 0)),
            ],
        ),
        out_shape=[
            jax.ShapeDtypeStruct((SEQ, width), F32),
            jax.ShapeDtypeStruct((SEQ, width), F32),
            jax.ShapeDtypeStruct((SEQ, width), F32),
            jax.ShapeDtypeStruct((HEADS, 8, SEQ), F32),
        ],
        compiler_params=pltpu.CompilerParams(vmem_limit_bytes=24 * 2**20),
        cost_estimate=pl.CostEstimate(
            flops=10 * SEQ * (cache + SEQ) * width,
            bytes_accessed=9 * 2**20,
            transcendentals=SEQ * (cache + SEQ) * HEADS,
        ),
        name="own",
    )(fill, q_own, grad, cache_k, cache_v, local_k, local_v)


def combine_kernel(x_ref, o_ref, a_ref, b_ref, s_ref, g_ref, att_ref, qg_ref, t_ref):
    g = g_ref[0].astype(F32)
    packed = x_ref[0, 3 * SEQ : 3 * SEQ + 32, :].astype(F32)
    rows = packed[0:8] + packed[8:16] + packed[16:24]
    mine = s_ref[0]
    tile = jnp.concatenate([rows, mine, jnp.zeros((SEQ - 16, SEQ), F32)], axis=0).T
    x_top, x_total, x_delta = tile[:, 0:1], tile[:, 1:2], tile[:, 2:3]
    o_top, o_total, o_delta = tile[:, 8:9], tile[:, 9:10], tile[:, 10:11]
    big = jnp.maximum(x_top, o_top)
    x_share = jnp.exp2(x_top - big)
    o_share = jnp.exp2(o_top - big)
    inverse = 1.0 / (x_share * x_total + o_share * o_total)
    x_weight = x_share * x_total * inverse
    o_weight = o_share * o_total * inverse
    attended = (x_weight * x_ref[0, 0:SEQ, :].astype(F32) + o_weight * o_ref[...]).astype(BF)
    delta = jnp.sum(g * attended.astype(F32), axis=1, keepdims=True)
    grad = x_weight * (
        x_ref[0, SEQ : 2 * SEQ, :].astype(F32)
        + (x_delta - delta) * x_ref[0, 2 * SEQ : 3 * SEQ, :].astype(F32)
    ) + o_weight * (a_ref[...] + (o_delta - delta) * b_ref[...])
    att_ref[0] = attended
    qg_ref[0] = (grad * SCALING).astype(BF)
    t_ref[0] = stat_rows([o_top, o_share * inverse, delta])[0:8, :]


def combine(returned, o, a, b, stats, grad):
    width = HEADS * HEAD
    block = pl.BlockSpec((SEQ, HEAD), lambda h: (0, h))
    row_block = pl.BlockSpec((1, SEQ, HEAD), lambda h: (0, 0, h))
    stat_block = pl.BlockSpec((1, 8, SEQ), lambda h: (h, 0, 0))
    return pl.pallas_call(
        combine_kernel,
        grid=(HEADS,),
        in_specs=[
            pl.BlockSpec((1, 3 * SEQ + 32, HEAD), lambda h: (h, 0, 0)),
            block,
            block,
            block,
            stat_block,
            row_block,
        ],
        out_specs=[
            row_block,
            pl.BlockSpec((1, SEQ, HEAD), lambda h: (h % 4, 0, h // 4)),
            stat_block,
        ],
        out_shape=[
            jax.ShapeDtypeStruct((1, SEQ, width), BF),
            jax.ShapeDtypeStruct((4, SEQ, 4 * HEAD), BF),
            jax.ShapeDtypeStruct((HEADS, 8, SEQ), F32),
        ],
        cost_estimate=pl.CostEstimate(
            flops=20 * SEQ * width, bytes_accessed=6 * 2**20, transcendentals=0
        ),
        name="combine",
    )(returned, o, a, b, stats, grad)


def local_kernel(t_ref, q_ref, g_ref, lk_ref, lv_ref, kg_ref, vg_ref):
    q = q_ref[0]
    g = g_ref[0]
    top, factor, delta = t_ref[0, 0:1, :], t_ref[0, 1:2, :], t_ref[0, 2:3, :]
    key = lax.broadcasted_iota(jnp.int32, (SEQ, SEQ), 0)
    query = lax.broadcasted_iota(jnp.int32, (SEQ, SEQ), 1)
    scores = jnp.where(key <= query, dot_nt(lk_ref[0], q) * (SCALING * LOG2E), NEG)
    prob = jnp.exp2(scores - top).astype(BF).astype(F32) * factor
    slope = (prob * (dot_nt(lv_ref[0], g) - delta)).astype(BF)
    vg_ref[0] = dot_nn(prob.astype(BF), g).astype(BF)
    kg_ref[0] = (dot_nn(slope, q) * SCALING).astype(BF)


def local_grads(stats, q_own, grad, local_k, local_v):
    width = HEADS * HEAD
    row_block = pl.BlockSpec((1, SEQ, HEAD), lambda h: (0, 0, h))
    return pl.pallas_call(
        local_kernel,
        grid=(HEADS,),
        in_specs=[
            pl.BlockSpec((1, 8, SEQ), lambda h: (h, 0, 0)),
            pl.BlockSpec((1, SEQ, HEAD), lambda h: (h % 4, 0, h // 4)),
            row_block,
            row_block,
            row_block,
        ],
        out_specs=[row_block, row_block],
        out_shape=[
            jax.ShapeDtypeStruct((1, SEQ, width), BF),
            jax.ShapeDtypeStruct((1, SEQ, width), BF),
        ],
        cost_estimate=pl.CostEstimate(
            flops=8 * SEQ * SEQ * width,
            bytes_accessed=3 * 2**20,
            transcendentals=SEQ * SEQ * HEADS,
        ),
        name="local",
    )(stats, q_own, grad, local_k, local_v)


def a2a(x, axis):
    return lax.all_to_all(x, axis, 0, 0, tiled=True)


def spread(x, count):
    return jnp.broadcast_to(x[None], (count,) + x.shape)


def body(
    tokens,
    query_weight,
    current_keys,
    current_values,
    cache_keys,
    cache_values,
    cache_fill,
    document_group,
    attended_grad,
):
    q_index = lax.axis_index("q")
    g_index = lax.axis_index("g")
    col_index = lax.axis_index(FS)
    shard_rows = query_weight.shape[0]

    quarter = lax.dynamic_index_in_dim(
        query_weight.reshape(shard_rows, 4, 4, HEAD), q_index, axis=2, keepdims=False
    ).reshape(shard_rows, 4 * HEAD)
    weight = a2a(spread(quarter, 16), FS).reshape(16 * shard_rows, 4 * HEAD)
    tok = a2a(spread(tokens[0], 4), "q").reshape(4 * SEQ, -1)

    kvg = jnp.stack(
        [
            x[0].reshape(SEQ, HEADS, HEAD).transpose(1, 0, 2)
            for x in (current_keys, current_values, attended_grad)
        ],
        axis=1,
    )
    kvg = a2a(kvg, XB)

    queries = jnp.dot(tok, weight, preferred_element_type=F32).astype(BF)
    by_head = queries.reshape(4 * SEQ, 4, HEAD).transpose(1, 0, 2)
    q_heads = a2a(by_head, "g").reshape(16, SEQ, HEAD)
    q_own = a2a(queries.reshape(4, SEQ, 4 * HEAD), "q")

    labels = lax.dynamic_index_in_dim(
        document_group.reshape(16, 16), col_index, axis=1, keepdims=False
    )
    number = jnp.arange(16)
    valid = (labels[:, None] == labels[None, :]) & (number[:, None] != number[None, :])
    bias = jnp.repeat(jnp.where(valid, 0.0, NEG).astype(F32), SEQ, axis=1)[:, None, :]

    returned = a2a(cross_attention(q_heads, kvg, bias), XB)
    o, a, b, stats = own_attention(
        cache_fill, q_own, attended_grad, cache_keys, cache_values, current_keys, current_values
    )
    attended, query_grad, stats = combine(returned, o, a, b, stats, attended_grad)

    qg = a2a(query_grad, "q").reshape(4 * SEQ, 4 * HEAD)
    partial = lax.dot_general(
        tok, qg, (((0,), (0,)), ((), ())), preferred_element_type=F32
    ).astype(BF)
    pieces = a2a(partial.reshape(16, shard_rows, 4 * HEAD), FS)
    mine = jnp.sum(pieces.astype(F32), axis=0).astype(BF)

    tokens_part = dot_nt(qg, weight).astype(BF).reshape(4, SEQ, -1)
    tokens_grad = jnp.sum(a2a(tokens_part, "q").astype(F32), axis=0, keepdims=True).astype(BF)
    keys_grad, values_grad = local_grads(stats, q_own, attended_grad, current_keys, current_values)

    summed = jnp.sum(a2a(spread(mine, 4), "g").astype(F32), axis=0).astype(BF)
    columns = a2a(spread(summed, 4), "q")
    weight_grad = (
        columns.reshape(4, shard_rows, 4, HEAD)
        .transpose(1, 2, 0, 3)
        .reshape(shard_rows, HEADS * HEAD)
        .astype(F32)
    )
    return attended, tokens_grad, keys_grad, values_grad, weight_grad


def solution(mesh):
    grid = Mesh(mesh.devices.reshape(4, 4, 4, 2, 2), XB + FS)
    docs = P(XB + FS, None, None)
    in_specs = (docs, P(FS, None), docs, docs, docs, docs, P(XB + FS), P(), docs)
    out_specs = (docs, docs, docs, docs, P(FS, None))
    return jax.shard_map(body, mesh=grid, in_specs=in_specs, out_specs=out_specs, check_vma=False)
```

time: 846 us -> 338 us (0.40)
  waiting for transfers between devices: 689 us -> 115 us
  blocking collectives: 0 us -> 76.3 us
  Pallas kernels: 0 us -> 59.1 us
  matrix products: 64.1 us -> 11.4 us
  starting transfers between devices: 0.19 us -> 41.4 us
  local copies, waits for them, and re-layouts: 65 us -> 23.9 us
  between operations: 14.6 us -> 1.51 us
    all_gather x3 -> x0, waiting for transfers between devices: 407 us -> none  [the longest x1 179 us: body(): lax.all_gather(current_keys, 'xb', axis=0, tiled=True)]
    reduce_scatter x1 -> x0, waiting for transfers between devices: 154 us -> none  [body(): lax.psum_scatter(jnp.einsum('tc,th->ch', inputs, query_grad, preferred_el...]
    psum x1 -> x0, waiting for transfers between devices: 126 us -> none  [body(): weight_grad = lax.psum(shard_rows, 'xb')]
    all_to_all x0 -> x8, waiting for transfers between devices: none -> 115 us  [a2a(): return lax.all_to_all(x, axis, 0, 0, tiled=True)]
    all_to_all x0 -> x3, blocking collectives: none -> 76.3 us  [a2a(): return lax.all_to_all(x, axis, 0, 0, tiled=True)]
    pallas_call x0 -> x4, Pallas kernels: none -> 59.1 us  [the longest x1 19.4 us: cross_attention(): pl.pallas_call(cross_kernel, grid=(docs // step,), in_specs=[pl.BlockSpec...]
    dot_general x15 -> x3, matrix products: 64.1 us -> 11.4 us  [the longest x1 4.31 us: body(): queries = jnp.dot(tok, weight, preferred_element_type=F32).astype(BF)]
    all_to_all x0 -> x8, starting transfers between devices: none -> 41.4 us  [a2a(): return lax.all_to_all(x, axis, 0, 0, tiled=True)]
  transfers between devices with their start and end apart: 5 -> 8, of which waited for: 5 -> 6; matrix products, arithmetic and copies ran while one was open for 7% -> 6% of each run, Pallas kernels for 0% -> 13%
where the time goes in v1:
time: 338 us; the launch traced here: 333 us
  waiting for transfers between devices  115 us (34%)
  blocking collectives  76.3 us (23%)
  Pallas kernels  59.1 us (17%)
  starting transfers between devices  41.4 us (12%)
  local copies, waits for them, and re-layouts  23.9 us (7%)
  matrix products  11.4 us (3%)
  other arithmetic  4.22 us (1%)
    all_to_all x8, waiting for transfers between devices, a2a(): return lax.all_to_all(x, axis, 0, 0, tiled=True)  115 us
    all_to_all x3, blocking collectives, a2a(): return lax.all_to_all(x, axis, 0, 0, tiled=True)  76.3 us
    all_to_all x8, starting transfers between devices, a2a(): return lax.all_to_all(x, axis, 0, 0, tiled=True)  41.4 us
    pallas_call x1, Pallas kernels, cross_attention(): pl.pallas_call(cross_kernel, grid=(docs // step,), in_specs=[pl.BlockSpec...  19.4 us
    pallas_call x1, Pallas kernels, combine(): pl.pallas_call(combine_kernel, grid=(HEADS,), in_specs=[pl.BlockSpec((1,...  14.8 us
    pallas_call x1, Pallas kernels, own_attention(): pl.pallas_call(own_kernel, grid_spec=pltpu.PrefetchScalarGridSpec(num_sca...  14.3 us
    unnamed x35, local copies, waits for them, and re-layouts  13.4 us
    pallas_call x1, Pallas kernels, local_grads(): pl.pallas_call(local_kernel, grid=(HEADS,), in_specs=[pl.BlockSpec((1, 8,...  10.6 us
  transfers between devices with their start and end apart: 8, of which 6 were waited for; matrix products, arithmetic and copies ran while one was open for 6% of the time, Pallas kernels for 13%

profile of v1, /device:TPU:48, one launch (start us, length us, event | category | flops | bytes accessed | tf_op | source)
XLA Modules:
  0.0 332.6 jit_solution(17896685985693499478)
XLA Ops:
  0.6 1.3 copy.56
  2.3 33.5 %all_to_all.55 = bf16[16,128,512]{2,1,0:T(8,128)(2,1)} all-to-all(bf16[16,128,512]{2,1,0:T(8,128)(2,1)S(1)} %broadcast_in_dim.23), channel_id=1, replica_groups=mesh['g'=4,'q'=4,'x'=4,'yh'=2,'core'=2] {'x','yh','core'}, dimensions={0} | all-to-all | bytes 4194304 | tf_op jit(solution)/shard_map/all_to_all | solution.py:290
  35.8 1.6 broadcast_in_dim.45
  37.4 4.6 %all-to-all-start.1 = ((bf16[4,128,2048]{2,1,0:T(8,128)(2,1)}), bf16[4,128,2048]{2,1,0:T(8,128)(2,1)}, u32[]{:S(2)}, u32[]{:S(2)}) async-start(bf16[4,128,2048]{2,1,0:T(8,128)(2,1)} %broadcast_in_dim.45), calls=%async_computation.1 | async-start | bytes 4194304 | tf_op jit(solution)/shard_map/all_to_all | solution.py:290
  44.9 2.4 pad_maximum_fusion
  47.3 19.8 %all-to-all-done.1 = bf16[4,128,2048]{2,1,0:T(8,128)(2,1)} async-done(((bf16[4,128,2048]{2,1,0:T(8,128)(2,1)}), bf16[4,128,2048]{2,1,0:T(8,128)(2,1)}, u32[]{:S(2)}, u32[]{:S(2)}) %all-to-all-start.1) | async-done | bytes 2097184 | tf_op jit(solution)/shard_map/all_to_all | solution.py:290
  67.1 10.0 %all-to-all-start.3 = ((bf16[16,3,128,128]{3,2,1,0:T(8,128)(2,1)}), bf16[16,3,128,128]{3,2,1,0:T(8,128)(2,1)S(1)}, u32[]{:S(2)}, u32[]{:S(2)}) async-start(bf16[16,3,128,128]{3,2,1,0:T(8,128)(2,1)} %pad_maximum_fusion), calls=%async_computation.3 | async-start | bytes 3145728 | tf_op jit(solution)/shard_map/all_to_all | solution.py:290
  77.1 4.3 %convolution_convert_fusion.1 = bf16[512,512]{1,0:T(8,128)(2,1)} fusion(bf16[2048,512]{1,0:T(8,128)(2,1)} %bitcast.52, bf16[512,2048]{1,0:T(8,128)(2,1)} %bitcast.4), kind=kOutput, calls=%fused_computation.5 | convolution fusion | flops 1074003968 | bytes 4718592 | tf_op jit(solution)/shard_map/dot_general | solution.py:328
  81.4 2.1 copy.58
  83.5 29.8 %all-to-all-done.3.kvg_ref.g_ref = bf16[16,3,128,128]{3,2,1,0:T(8,128)(2,1)S(1)} async-done(((bf16[16,3,128,128]{3,2,1,0:T(8,128)(2,1)}), bf16[16,3,128,128]{3,2,1,0:T(8,128)(2,1)S(1)}, u32[]{:S(2)}, u32[]{:S(2)}) %all-to-all-start.3) | async-done | bytes 1572896 | tf_op jit(solution)/shard_map/all_to_all | solution.py:290
  113.3 4.8 %all-to-all-start.2 = ((bf16[4,512,128]{2,1,0:T(8,128)(2,1)}), bf16[4,512,128]{2,1,0:T(8,128)(2,1)}, u32[]{:S(2)}, u32[]{:S(2)}) async-start(bf16[4,512,128]{2,1,0:T(8,128)(2,1)} %bitcast.58), calls=%async_computation.2 | async-start | bytes 1048576 | tf_op jit(solution)/shard_map/all_to_all | solution.py:290
  118.1 2.0 copy.65
  120.1 14.1 %all-to-all-done.2 = bf16[4,512,128]{2,1,0:T(8,128)(2,1)} async-done(((bf16[4,512,128]{2,1,0:T(8,128)(2,1)}), bf16[4,512,128]{2,1,0:T(8,128)(2,1)}, u32[]{:S(2)}, u32[]{:S(2)}) %all-to-all-start.2) | async-done | bytes 524320 | tf_op jit(solution)/shard_map/all_to_all | solution.py:290
  134.2 4.1 %all-to-all-start.5 = ((bf16[4,128,512]{2,1,0:T(8,128)(2,1)}), bf16[4,128,512]{2,1,0:T(8,128)(2,1)S(1)}, u32[]{:S(2)}, u32[]{:S(2)}) async-start(bf16[4,128,512]{2,1,0:T(8,128)(2,1)} %bitcast.55), calls=%async_computation.5 | async-start | bytes 1048576 | tf_op jit(solution)/shard_map/all_to_all | solution.py:290
  138.7 1.4 copy-done.8
  140.1 19.4 %cross.1 = bf16[16,416,128]{2,1,0:T(8,128)(2,1)S(1)} custom-call(bf16[16,128,128]{2,1,0:T(8,128)(2,1)} %bitcast.8.q_ref, bf16[16,3,128,128]{3,2,1,0:T(8,128)(2,1)S(1)} %copy-done.8, bf16[16,3,128,128]{3,2,1,0:T(8,128)(2,1)S(1)} %copy-done.8, f32[16,1,2048]{2,1,0:T(1,128)S(1)} %bitcast.48), custom_call_target="tpu_custom_call" | custom-call | flops 5368709120 | bytes 4194304 | tf_op jit(solution)/shard_map/cross/pallas_call | solution.py:92
  160.7 5.5 %all-to-all-start.4 = ((bf16[16,416,128]{2,1,0:T(8,128)(2,1)}), bf16[16,416,128]{2,1,0:T(8,128)(2,1)}, u32[]{:S(2)}, u32[]{:S(2)}) async-start(bf16[16,416,128]{2,1,0:T(8,128)(2,1)} %copy-done.6), calls=%async_computation.4 | async-start | bytes 3407872 | tf_op jit(solution)/shard_map/all_to_all | solution.py:290
  166.8 1.6 copy-done.4
  168.4 1.6 copy-done.5
  170.0 14.3 %own.1 = (f32[128,2048]{1,0:T(8,128)S(1)}, f32[128,2048]{1,0:T(8,128)S(1)}, f32[128,2048]{1,0:T(8,128)S(1)}, f32[16,8,128]{2,1,0:T(8,128)S(1)}) custom-call(s32[1]{0:T(128)S(6)} %copy.78.fill_ref, bf16[4,128,512]{2,1,0:T(8,128)(2,1)S(1)} %all-to-all-done.5.q_ref, bf16[1,128,2048]{2,1,0:T(8,128)(2,1)S(1)} %copy-done, bf16[1,512,2048]{2,1,0:T(8,128)(2,1)S(1)} %copy-done.4, ...), custom_call_target="tpu_custom_call" | custom-call | flops 1677721600 | bytes 9437184 | tf_op jit(solution)/shard_map/own/pallas_call | solution.py:155
  188.0 16.2 %all-to-all-done.4.x_ref = bf16[16,416,128]{2,1,0:T(8,128)(2,1)} async-done(((bf16[16,416,128]{2,1,0:T(8,128)(2,1)}), bf16[16,416,128]{2,1,0:T(8,128)(2,1)}, u32[]{:S(2)}, u32[]{:S(2)}) %all-to-all-start.4) | async-done | bytes 1703968 | tf_op jit(solution)/shard_map/all_to_all | solution.py:290
  204.2 14.8 %combine.1 = (bf16[1,128,2048]{2,1,0:T(8,128)(2,1)}, bf16[4,128,512]{2,1,0:T(8,128)(2,1)}, f32[16,8,128]{2,1,0:T(8,128)}) custom-call(bf16[16,416,128]{2,1,0:T(8,128)(2,1)} %all-to-all-done.4.x_ref, f32[128,2048]{1,0:T(8,128)} %copy-done.9, f32[128,2048]{1,0:T(8,128)} %copy-done.10, f32[128,2048]{1,0:T(8,128)} %copy-done.11, f32[16,8,128]{2,1,0:T(8,128)} %copy-done.12, ...), custom_call_target="tpu_custom_call" | custom-call | flops 5242880 | bytes 6291456 | tf_op jit(solution)/shard_map/combine/pallas_call | solution.py:221
  219.0 11.6 %all_to_all.56 = bf16[4,128,512]{2,1,0:T(8,128)(2,1)S(1)} all-to-all(bf16[4,128,512]{2,1,0:T(8,128)(2,1)} %get-tuple-element.19), channel_id=1, replica_groups=mesh['g'=4,'q'=4,'x'=4,'yh'=2,'core'=2] {'q'}, dimensions={0} | all-to-all | bytes 1048576 | tf_op jit(solution)/shard_map/all_to_all | solution.py:290
  230.6 2.9 fusion
  234.0 31.2 %all_to_all.57 = bf16[16,128,512]{1,2,0:T(8,128)(2,1)S(1)} all-to-all(bf16[16,128,512]{1,2,0:T(8,128)(2,1)S(1)} %bitcast.49), channel_id=1, replica_groups=mesh['g'=4,'q'=4,'x'=4,'yh'=2,'core'=2] {'x','yh','core'}, dimensions={0} | all-to-all | bytes 4194304 | tf_op jit(solution)/shard_map/all_to_all | solution.py:290
  266.5 4.3 %all-to-all-start.9 = ((bf16[4,128,512]{2,1,0:T(8,128)(2,1)}), bf16[4,128,512]{2,1,0:T(8,128)(2,1)S(1)}, u32[]{:S(2)}, u32[]{:S(2)}) async-start(bf16[4,128,512]{2,1,0:T(8,128)(2,1)} %broadcast_in_dim.49), calls=%async_computation.9 | async-start | bytes 1048576 | tf_op jit(solution)/shard_map/all_to_all | solution.py:290
  270.8 4.2 %convolution_convert_fusion = bf16[512,2048]{1,0:T(8,128)(2,1)} fusion(bf16[512,512]{1,0:T(8,128)(2,1)S(1)} %bitcast.67, bf16[2048,512]{1,0:T(8,128)(2,1)} %bitcast.53), kind=kOutput, calls=%fused_computation.1 | convolution fusion | flops 1074790400 | bytes 4718592 | tf_op jit(solution)/shard_map/dot_general | solution.py:25
  275.0 12.8 %all-to-all-done.9 = bf16[4,128,512]{2,1,0:T(8,128)(2,1)S(1)} async-done(((bf16[4,128,512]{2,1,0:T(8,128)(2,1)}), bf16[4,128,512]{2,1,0:T(8,128)(2,1)S(1)}, u32[]{:S(2)}, u32[]{:S(2)}) %all-to-all-start.9) | async-done | bytes 524320 | tf_op jit(solution)/shard_map/all_to_all | solution.py:290
  287.8 3.6 %all-to-all-start.7 = ((bf16[4,128,2048]{2,1,0:T(8,128)(2,1)}), bf16[4,128,2048]{2,1,0:T(8,128)(2,1)S(1)}, u32[]{:S(2)}, u32[]{:S(2)}) async-start(bf16[4,128,2048]{2,1,0:T(8,128)(2,1)} %bitcast.54), calls=%async_computation.7 | async-start | bytes 4194304 | tf_op jit(solution)/shard_map/all_to_all | solution.py:290
  291.6 22.2 %all-to-all-done.7 = bf16[4,128,2048]{2,1,0:T(8,128)(2,1)S(1)} async-done(((bf16[4,128,2048]{2,1,0:T(8,128)(2,1)}), bf16[4,128,2048]{2,1,0:T(8,128)(2,1)S(1)}, u32[]{:S(2)}, u32[]{:S(2)}) %all-to-all-start.7) | async-done | bytes 2097184 | tf_op jit(solution)/shard_map/all_to_all | solution.py:290
  314.7 4.5 %all-to-all-start.10 = ((bf16[4,128,512]{1,2,0:T(8,128)(2,1)}), bf16[4,128,512]{1,2,0:T(8,128)(2,1)S(1)}, u32[]{:S(2)}, u32[]{:S(2)}) async-start(bf16[4,128,512]{1,2,0:T(8,128)(2,1)} %broadcast_in_dim.50), calls=%async_computation.10 | async-start | bytes 1048576 | tf_op jit(solution)/shard_map/all_to_all | solution.py:290
  319.2 10.6 %local.1 = (bf16[1,128,2048]{2,1,0:T(8,128)(2,1)}, bf16[1,128,2048]{2,1,0:T(8,128)(2,1)}) custom-call(f32[16,8,128]{2,1,0:T(8,128)} %get-tuple-element.20.t_ref, bf16[4,128,512]{2,1,0:T(8,128)(2,1)} %copy-done.3, bf16[1,128,2048]{2,1,0:T(8,128)(2,1)} %g_ref.5, bf16[1,128,2048]{2,1,0:T(8,128)(2,1)} %lk_ref.3, bf16[1,128,2048]{2,1,0:T(8,128)(2,1)} %lv_ref.3), custom_call_target="tpu_custom_call" | custom-call | flops 268435456 | bytes 3145728 | tf_op jit(solution)/shard_map/local/pallas_call | solution.py:265
  (53 shorter events, 14.1 us)
Async XLA Ops:
  2.3 33.5 %copy-start.13 = (bf16[1,128,2048]{2,1,0:T(8,128)(2,1)S(1)}, bf16[1,128,2048]{2,1,0:T(8,128)(2,1)}, u32[]{:S(2)}) copy-start(bf16[1,128,2048]{2,1,0:T(8,128)(2,1)} %param.9) | copy-start | bytes 1572868
  37.4 4.6 %copy-start.2 = (bf16[1,128,2048]{2,1,0:T(8,128)(2,1)S(1)}, bf16[1,128,2048]{2,1,0:T(8,128)(2,1)}, u32[]{:S(2)}) copy-start(bf16[1,128,2048]{2,1,0:T(8,128)(2,1)} %lk_ref.3) | copy-start | bytes 1572868
  37.4 29.7 %all-to-all-start.1 = ((bf16[4,128,2048]{2,1,0:T(8,128)(2,1)}), bf16[4,128,2048]{2,1,0:T(8,128)(2,1)}, u32[]{:S(2)}, u32[]{:S(2)}) async-start(bf16[4,128,2048]{2,1,0:T(8,128)(2,1)} %broadcast_in_dim.45), calls=%async_computation.1 | async-start | bytes 4194304 | tf_op jit(solution)/shard_map/all_to_all | solution.py:290
  42.0 1.0 copy-start.1
  42.0 1.6 copy-start
  67.1 46.1 %all-to-all-start.3 = ((bf16[16,3,128,128]{3,2,1,0:T(8,128)(2,1)}), bf16[16,3,128,128]{3,2,1,0:T(8,128)(2,1)S(1)}, u32[]{:S(2)}, u32[]{:S(2)}) async-start(bf16[16,3,128,128]{3,2,1,0:T(8,128)(2,1)} %pad_maximum_fusion), calls=%async_computation.3 | async-start | bytes 3145728 | tf_op jit(solution)/shard_map/all_to_all | solution.py:290
  81.4 56.8 %copy-start.14 = (s32[256]{0:T(256)S(1)}, s32[256]{0:T(256)}, u32[]{:S(2)}) copy-start(s32[256]{0:T(256)} %param.16) | copy-start | bytes 3076
  113.3 20.9 %copy-start.7 = (bf16[16,3,128,128]{3,2,1,0:T(8,128)(2,1)}, bf16[16,3,128,128]{3,2,1,0:T(8,128)(2,1)S(1)}, u32[]{:S(2)}) copy-start(bf16[16,3,128,128]{3,2,1,0:T(8,128)(2,1)S(1)} %all-to-all-done.3.kvg_ref.g_ref) | copy-start | bytes 4718596
  113.3 20.9 %all-to-all-start.2 = ((bf16[4,512,128]{2,1,0:T(8,128)(2,1)}), bf16[4,512,128]{2,1,0:T(8,128)(2,1)}, u32[]{:S(2)}, u32[]{:S(2)}) async-start(bf16[4,512,128]{2,1,0:T(8,128)(2,1)} %bitcast.58), calls=%async_computation.2 | async-start | bytes 1048576 | tf_op jit(solution)/shard_map/all_to_all | solution.py:290
  134.2 26.5 %all-to-all-start.5 = ((bf16[4,128,512]{2,1,0:T(8,128)(2,1)}), bf16[4,128,512]{2,1,0:T(8,128)(2,1)S(1)}, u32[]{:S(2)}, u32[]{:S(2)}) async-start(bf16[4,128,512]{2,1,0:T(8,128)(2,1)} %bitcast.55), calls=%async_computation.5 | async-start | bytes 1048576 | tf_op jit(solution)/shard_map/all_to_all | solution.py:290
  138.7 1.4 copy-start.8
  159.5 1.2 copy-start.6
  160.7 23.7 %copy-start.3 = (bf16[4,128,512]{2,1,0:T(8,128)(2,1)}, bf16[4,128,512]{2,1,0:T(8,128)(2,1)S(1)}, u32[]{:S(2)}) copy-start(bf16[4,128,512]{2,1,0:T(8,128)(2,1)S(1)} %all-to-all-done.5.q_ref) | copy-start | bytes 1572868
  160.7 43.5 %all-to-all-start.4 = ((bf16[16,416,128]{2,1,0:T(8,128)(2,1)}), bf16[16,416,128]{2,1,0:T(8,128)(2,1)}, u32[]{:S(2)}, u32[]{:S(2)}) async-start(bf16[16,416,128]{2,1,0:T(8,128)(2,1)} %copy-done.6), calls=%async_computation.4 | async-start | bytes 3407872 | tf_op jit(solution)/shard_map/all_to_all | solution.py:290
  166.8 1.6 copy-start.4
  168.4 1.6 copy-start.5
  184.3 1.0 copy-start.9
  185.3 1.1 copy-start.10
  186.4 1.0 copy-start.11
  187.4 0.6 copy-start.12
  266.5 21.4 %all-to-all-start.9 = ((bf16[4,128,512]{2,1,0:T(8,128)(2,1)}), bf16[4,128,512]{2,1,0:T(8,128)(2,1)S(1)}, u32[]{:S(2)}, u32[]{:S(2)}) async-start(bf16[4,128,512]{2,1,0:T(8,128)(2,1)} %broadcast_in_dim.49), calls=%async_computation.9 | async-start | bytes 1048576 | tf_op jit(solution)/shard_map/all_to_all | solution.py:290
  287.8 26.0 %all-to-all-start.7 = ((bf16[4,128,2048]{2,1,0:T(8,128)(2,1)}), bf16[4,128,2048]{2,1,0:T(8,128)(2,1)S(1)}, u32[]{:S(2)}, u32[]{:S(2)}) async-start(bf16[4,128,2048]{2,1,0:T(8,128)(2,1)} %bitcast.54), calls=%async_computation.7 | async-start | bytes 4194304 | tf_op jit(solution)/shard_map/all_to_all | solution.py:290
  314.7 16.4 %all-to-all-start.10 = ((bf16[4,128,512]{1,2,0:T(8,128)(2,1)}), bf16[4,128,512]{1,2,0:T(8,128)(2,1)S(1)}, u32[]{:S(2)}, u32[]{:S(2)}) async-start(bf16[4,128,512]{1,2,0:T(8,128)(2,1)} %broadcast_in_dim.50), calls=%async_computation.10 | async-start | bytes 1048576 | tf_op jit(solution)/shard_map/all_to_all | solution.py:290
